TPU v7x, 32 devices: a whole 2x2x4 slice. The times are simulated.
32 devices in a mesh: groups: 2 (over y), seq: 4 (over x, core), head: 4 (over z).
Axes of the slice: x: 2, y: 2, z: 4, core: 2. Of those that a mesh axis runs over, the one named last changes fastest.
Arguments:
- queries: bfloat16 [2048, 64, 128], P(('groups', 'seq'), 'head'), parts along dimension 0, may hold values from -40 to 40
- seq_keys: bfloat16 [2048, 8, 128], P(('groups', 'seq'), 'head'), parts along dimension 0, may hold values from -6 to 6
- seq_values: bfloat16 [2048, 8, 128], P(('groups', 'seq'), 'head'), parts along dimension 0, may hold values from -6 to 6
- out_grad: bfloat16 [2048, 64, 128], P(('groups', 'seq'), 'head'), parts along dimension 0, may hold values from -6 to 6
- prefix_keys: bfloat16 [64, 8, 128], P(None, 'head'), may hold values from -6 to 6
- prefix_values: bfloat16 [64, 8, 128], P(None, 'head'), may hold values from -6 to 6
- global_ids: int32 [4], P('groups'), parts along dimension 0, may hold values from 0 to 7
- rand_owner: int32 [16, 2], P(('groups', 'seq')), parts along dimension 0, may hold values from 0 to 3, as said below
- rand_offset: int32 [16, 2], P(('groups', 'seq')), parts along dimension 0, may hold values from 0 to 1
- doc_length: int32 [2], P('groups'), parts along dimension 0, may hold values from 512 to 1024
Outputs:
- attn_out: bfloat16 [2048, 64, 128], P(('groups', 'seq'), 'head'), parts along dimension 0
- grad_queries: bfloat16 [2048, 64, 128], P(('groups', 'seq'), 'head'), parts along dimension 0
- grad_seq_keys: bfloat16 [2048, 8, 128], P(('groups', 'seq'), 'head'), parts along dimension 0
- grad_seq_values: bfloat16 [2048, 8, 128], P(('groups', 'seq'), 'head'), parts along dimension 0
- grad_prefix_keys: float32 [128, 8, 128], P('groups', 'head'), parts along dimension 0
- grad_prefix_values: float32 [128, 8, 128], P('groups', 'head'), parts along dimension 0
There are 2 independent parts, one for each index of `groups`. A program takes and returns all parts, laid end to end along the dimension named above; an argument that names none is the same for every part. Nothing has to cross between parts.
Inputs may be any that keep to these rules, and one draw needn't show every extreme that they name: `rand_owner`: each row names 2 different indices; the 2 rows of one index of seq name any one index at most 2 times, and some index exactly 2 times.
All inputs are finite; a program needn't handle non-finite values.
Results may differ from a plain program's by a relative error of at most 0.0055.
Values may be sent and summed in bfloat16 or wider, within the bound.
A program may use at most 128 MiB of HBM per device.

v0:
```python
import math

import jax
import jax.numpy as jnp
from jax import lax
from jax.sharding import PartitionSpec as P

BLK = 128
P_SIZE = 64
S_DEV = 256


masked_score = -1e30


def block_list(query_rows, global_ids, rand_owner, rand_offset):
    count_rows = query_rows.shape[0]
    window = jnp.stack([query_rows - 1, query_rows], axis=1)
    globals_all = jnp.broadcast_to(global_ids[None, :], (count_rows, global_ids.shape[0]))
    randoms = rand_owner * (S_DEV // BLK) + rand_offset
    return jnp.concatenate([window, globals_all, randoms], axis=1)


def build_masks(query_rows, key_blocks, length):
    slot_count = key_blocks.shape[1]
    earlier_slot = jnp.arange(slot_count)[None, :] < jnp.arange(slot_count)[:, None]
    repeated = jnp.any(
        (key_blocks[:, :, None] == key_blocks[:, None, :]) & earlier_slot[None], axis=2
    )
    allowed = (key_blocks >= 0) & (key_blocks <= query_rows[:, None]) & jnp.logical_not(repeated)
    within = jnp.arange(BLK, dtype=jnp.int32)
    key_pos = key_blocks[:, :, None] * BLK + within[None, None, :]
    query_pos = query_rows[:, None] * BLK + within[None, :]
    visible = (
        allowed[:, None, :, None]
        & (key_pos[:, None] <= query_pos[:, :, None, None])
        & (key_pos[:, None] < length)
    )
    visible = visible.reshape(query_rows.shape[0], BLK, slot_count * BLK)
    prefix_cols = jnp.ones((query_rows.shape[0], BLK, P_SIZE), dtype=jnp.bool_)
    return (jnp.concatenate([prefix_cols, visible], axis=2), query_pos < length)


def attend(query_blk, grad_blk, key_rows, value_rows, visible, query_valid):
    scaling = 1.0 / math.sqrt(query_blk.shape[-1])
    scores = (
        jnp.einsum("tgqd,kgd->gqtk", query_blk, key_rows, preferred_element_type=jnp.float32)
        * scaling
    )
    scores = jnp.where(visible[None, None], scores, masked_score)
    maxima = jnp.max(scores, axis=-1, keepdims=True)
    weights = jnp.where(visible[None, None], jnp.exp(scores - maxima), 0.0)
    probability = weights / jnp.sum(weights, axis=-1, keepdims=True)
    prob_bf = probability.astype(jnp.bfloat16)
    valid_col = query_valid[:, None, None, None]
    mixed = jnp.einsum("gqtk,kgd->tgqd", prob_bf, value_rows, preferred_element_type=jnp.float32)
    attn_out = jnp.where(valid_col, mixed, 0.0).astype(jnp.bfloat16)
    masked_grad = jnp.where(valid_col, grad_blk, jnp.zeros_like(grad_blk))
    grad_prob = jnp.einsum(
        "tgqd,kgd->gqtk", masked_grad, value_rows, preferred_element_type=jnp.float32
    )
    row_delta = jnp.sum(probability * grad_prob, axis=-1, keepdims=True)
    grad_score = (probability * (grad_prob - row_delta)).astype(jnp.bfloat16)
    grad_query = (
        scaling
        * jnp.einsum("gqtk,kgd->tgqd", grad_score, key_rows, preferred_element_type=jnp.float32)
    ).astype(jnp.bfloat16)
    grad_keys = scaling * jnp.einsum(
        "gqtk,tgqd->kgd", grad_score, query_blk, preferred_element_type=jnp.float32
    )
    grad_values = jnp.einsum(
        "gqtk,tgqd->kgd", prob_bf, masked_grad, preferred_element_type=jnp.float32
    )
    return (attn_out, grad_query, grad_keys, grad_values)


def on_device(
    queries,
    seq_keys,
    seq_values,
    out_grad,
    prefix_keys,
    prefix_values,
    global_ids,
    rand_owner,
    rand_offset,
    doc_length,
):
    devices = lax.axis_size("seq")
    device = lax.axis_index("seq")
    per_dev = seq_keys.shape[0] // BLK
    groups = seq_keys.shape[1]
    width = seq_keys.shape[2]
    qheads = queries.shape[1] // groups
    query_rows = device * per_dev + jnp.arange(per_dev, dtype=jnp.int32)
    key_blocks = block_list(query_rows, global_ids, rand_owner, rand_offset)
    key_masks, query_valid = build_masks(query_rows, key_blocks, doc_length[0])
    slot_count = key_blocks.shape[1]
    safe_index = jnp.maximum(key_blocks, 0)
    whole_keys, whole_values = (
        lax.all_gather(seq_keys, "seq", axis=0, tiled=True),
        lax.all_gather(seq_values, "seq", axis=0, tiled=True),
    )
    listed_keys = whole_keys.reshape(-1, BLK, groups, width)[safe_index]
    listed_values = whole_values.reshape(-1, BLK, groups, width)[safe_index]
    query_tiles = queries.reshape(per_dev, BLK, groups, qheads, width)
    grad_tiles = out_grad.reshape(per_dev, BLK, groups, qheads, width)

    def one_block(block_item):
        query_blk, grad_blk, keys_blk, values_blk, visible, valid_blk = block_item
        key_rows = jnp.concatenate([prefix_keys, keys_blk.reshape(-1, groups, width)], axis=0)
        value_rows = jnp.concatenate([prefix_values, values_blk.reshape(-1, groups, width)], axis=0)
        return attend(query_blk, grad_blk, key_rows, value_rows, visible, valid_blk)

    attn_out, grad_query, grad_keys, grad_values = lax.map(
        one_block, (query_tiles, grad_tiles, listed_keys, listed_values, key_masks, query_valid)
    )
    prefix_gk = jnp.sum(grad_keys[:, :P_SIZE], axis=0)
    prefix_gv = jnp.sum(grad_values[:, :P_SIZE], axis=0)
    slot_gk = grad_keys[:, P_SIZE:].reshape(per_dev, slot_count, BLK, groups, width)
    slot_gv = grad_values[:, P_SIZE:].reshape(per_dev, slot_count, BLK, groups, width)
    full_keys = (
        jnp.zeros((devices * per_dev, BLK, groups, width), jnp.float32)
        .at[safe_index.reshape(-1)]
        .add(slot_gk.reshape(-1, BLK, groups, width))
    )
    full_values = (
        jnp.zeros((devices * per_dev, BLK, groups, width), jnp.float32)
        .at[safe_index.reshape(-1)]
        .add(slot_gv.reshape(-1, BLK, groups, width))
    )
    local_keys, local_values = (
        lax.psum_scatter(full_keys, "seq", scatter_dimension=0, tiled=True),
        lax.psum_scatter(full_values, "seq", scatter_dimension=0, tiled=True),
    )
    prefix_keys_all, prefix_values_all = lax.psum((prefix_gk, prefix_gv), "seq")
    token_count = per_dev * BLK
    return (
        attn_out.reshape(token_count, groups * qheads, width),
        grad_query.reshape(token_count, groups * qheads, width),
        local_keys.reshape(token_count, groups, width).astype(jnp.bfloat16),
        local_values.reshape(token_count, groups, width).astype(jnp.bfloat16),
        prefix_keys_all,
        prefix_values_all,
    )


def solution(mesh):
    placed = (
        P(("groups", "seq"), "head", None),
        P(("groups", "seq"), "head", None),
        P(("groups", "seq"), "head", None),
        P(("groups", "seq"), "head", None),
        P(None, "head", None),
        P(None, "head", None),
        P("groups"),
        P(("groups", "seq"), None),
        P(("groups", "seq"), None),
        P("groups"),
    )
    return jax.shard_map(
        on_device,
        mesh=mesh,
        in_specs=placed,
        out_specs=(
            P(("groups", "seq"), "head", None),
            P(("groups", "seq"), "head", None),
            P(("groups", "seq"), "head", None),
            P(("groups", "seq"), "head", None),
            P("groups", "head", None),
            P("groups", "head", None),
        ),
        check_vma=False,
    )
```

profile of v0, /device:TPU:0, one launch (start us, length us, event | category | flops | bytes accessed | tf_op | source)
XLA Modules:
  0.0 212.1 jit_solution(15392441976242258493)
XLA Ops:
  10.7 0.9 copy.128
  11.7 8.6 %all_gather.6 = bf16[1024,2,128]{2,0,1:T(8,128)(2,1)S(1)} all-gather(bf16[256,2,128]{2,0,1:T(8,128)(2,1)S(1)} %copy.128), channel_id=1, replica_groups=mesh['groups'=2,'seq'=4,'head'=4] {'seq'}, dimensions={0}, use_global_device_ids=true | all-gather | bytes 655360 | tf_op jit(solution)/shard_map/all_gather | solution.py:102
  20.4 0.9 copy.132
  21.3 7.3 %all_gather.7 = bf16[1024,2,128]{2,0,1:T(8,128)(2,1)S(1)} all-gather(bf16[256,2,128]{2,0,1:T(8,128)(2,1)S(1)} %copy.132), channel_id=1, replica_groups=mesh['groups'=2,'seq'=4,'head'=4] {'seq'}, dimensions={0}, use_global_device_ids=true | all-gather | bytes 655360 | tf_op jit(solution)/shard_map/all_gather | solution.py:101
  30.2 1.0 and_and_fusion
  31.2 82.0 %while.16 = (s32[]{:T(128)}, bf16[2,128,2,8,128]{4,3,2,1,0:T(8,128)(2,1)}, bf16[2,128,2,8,128]{4,3,2,1,0:T(8,128)(2,1)}, f32[2,832,2,128]{3,1,2,0:T(8,128)}, f32...) while((s32[]{:T(128)}, ...), condition=%wide.region_5.6_spmd, body=%wide.region_1.5_spmd.sunk | while | flops 2649701120 | bytes 120048320 | solution.py:115
  31.2 0.9 copy-done.10
  32.2 1.2 constant_dynamic-slice_fusion.9
  33.4 4.6 %fusion.75 = (f32[2,8,128]{2,1,0:T(8,128)S(1)}, f32[2,8,128,832]{2,3,1,0:T(8,128)}) fusion(pred[128,832]{0,1:T(8,128)(4,1)S(1)} %dynamic-slice_bitcast_fusion.2, bf16[1,128,2,8,128]{4,3,2,1,0:T(8,128)(2,1)S(1)} %constant_dynamic-slice_fusion.9, bf16[768,2,128]{2,0,1:T(8,128)(2,1)S(1)} %bitcast.182, bf16[64,2,128]{2,0,1:T(8,128)(2,1)S(1)} %get-tuple-element.380), kind=kOutput, calls=%fused_computation.85.clone.1 | convolution fusion | flops 445580096 | bytes 7880704 | tf_op jit(solution)/shard_map/while/body/eval_jaxpr/sub | solution.py:52
  38.2 1.2 constant_dynamic-slice_fusion.11
  39.4 7.1 %fusion.77 = (f32[2,8,128]{2,1,0:T(8,128)S(1)}, f32[2,832,128,8]{2,1,3,0:T(8,128)}) fusion(f32[2,8,128,832]{2,3,1,0:T(8,128)} %get-tuple-element.336, f32[2,8,128]{2,1,0:T(8,128)S(1)} %get-tuple-element.337, bf16[1,128,2,8,128]{4,3,2,1,0:T(8,128)(2,1)S(1)} %constant_dynamic-slice_fusion.11, pred[128]{0:T(512)(128)(4,1)S(1)} %fusion.76, ...), kind=kOutput, calls=%fused_computation.7.clone.1 | convolution fusion | flops 442431488 | bytes 14598272 | tf_op jit(solution)/shard_map/while/body/eval_jaxpr/tgqd,kgd->gqtk/dot_general | solution.py:59
  46.6 4.2 %fusion.78 = bf16[2,8,128,832]{2,3,1,0:T(8,128)(2,1)S(1)} fusion(f32[2,832,128,8]{2,1,3,0:T(8,128)} %get-tuple-element.338, f32[2,8,128]{2,1,0:T(8,128)S(1)} %get-tuple-element.339, f32[2,8,128,832]{2,3,1,0:T(8,128)S(1)} %bitcast.181, f32[2,8,128]{2,1,0:T(8,128)S(1)} %get-tuple-element.337), kind=kLoop, calls=%fused_computation.9.clone.1 | loop fusion | flops 6815744 | bytes 17055744 | tf_op jit(solution)/shard_map/while/body/eval_jaxpr/convert_element_type | solution.py:63
  50.8 1.6 fusion.79
  52.4 2.2 %copy.203 = bf16[1,128,2,8,128]{4,3,2,1,0:T(8,128)(2,1)} copy(bf16[1,128,2,8,128]{1,4,3,2,0:T(8,128)(2,1)} %fusion.79) | data formatting | bytes 1048576 | tf_op jit(solution)/shard_map/while/body/jit(dynamic_update_index_in_dim)/dynamic_update_slice | solution.py:115
  54.6 4.7 %fusion.80 = bf16[1,128,2,8,128]{1,4,3,2,0:T(8,128)(2,1)} fusion(pred[128]{0:T(512)(128)(4,1)S(1)} %fusion.76, bf16[768,2,128]{2,0,1:T(8,128)(2,1)} %bitcast.185, bf16[64,2,128]{2,0,1:T(8,128)(2,1)S(1)} %get-tuple-element.377, f32[2,8,128,832]{2,3,1,0:T(8,128)} %get-tuple-element.336, f32[2,8,128]{2,1,0:T(8,128)S(1)} %get-tuple-element.337), kind=kOutput, calls=%fused_computation.31.clone.1 | convolution fusion | flops 440991744 | bytes 7774336 | tf_op jit(solution)/shard_map/while/body/eval_jaxpr/gqtk,kgd->tgqd/dot_general | solution.py:56
  59.3 2.3 %copy.204 = bf16[1,128,2,8,128]{4,3,2,1,0:T(8,128)(2,1)} copy(bf16[1,128,2,8,128]{1,4,3,2,0:T(8,128)(2,1)} %fusion.80) | data formatting | bytes 1048576 | tf_op jit(solution)/shard_map/while/body/jit(dynamic_update_index_in_dim)/dynamic_update_slice | solution.py:115
  61.6 2.4 %constant_dynamic-update-slice_fusion.3 = (bf16[2,128,2,8,128]{4,3,2,1,0:T(8,128)(2,1)}, bf16[2,128,2,8,128]{4,3,2,1,0:T(8,128)(2,1)}) fusion(bf16[2,128,2,8,128]{4,3,2,1,0:T(8,128)(2,1)} %get-tuple-element.358, bf16[1,128,2,8,128]{4,3,2,1,0:T(8,128)(2,1)} %copy.203, s32[]{:T(128)} %get-tuple-element.356, ...), kind=kLoop, calls=%fused_computation.42.clone.1 | loop fusion | bytes 2097664 | tf_op jit(solution)/shard_map/while/body/jit(dynamic_update_index_in_dim)/dynamic_update_slice | solution.py:115
  64.0 3.0 %fusion.81 = f32[2,832,2,128]{3,1,2,0:T(8,128)} fusion(f32[2,832,2,128]{3,1,2,0:T(8,128)} %get-tuple-element.359, s32[]{:T(128)} %get-tuple-element.356, bf16[2,8,128,832]{2,3,1,0:T(8,128)(2,1)S(1)} %fusion.78, bf16[1,128,2,8,128]{4,3,2,1,0:T(8,128)(2,1)} %copy-done), kind=kOutput, calls=%fused_computation.28.clone.1 | convolution fusion | flops 436420608 | bytes 4784640 | tf_op jit(solution)/shard_map/while/body/eval_jaxpr/gqtk,tgqd->kgd/dot_general | solution.py:68
  67.0 5.1 %fusion.82 = f32[2,832,2,128]{3,1,2,0:T(8,128)} fusion(f32[2,832,2,128]{3,1,2,0:T(8,128)} %get-tuple-element.360, s32[]{:T(128)} %get-tuple-element.356, bf16[1,128,2,8,128]{4,3,2,1,0:T(8,128)(2,1)S(1)} %copy-done.4, pred[128]{0:T(512)(128)(4,1)S(1)} %fusion.76, f32[2,8,128,832]{2,3,1,0:T(8,128)} %get-tuple-element.336, ...), kind=kOutput, calls=%fused_computation.24.clone.1 | convolution fusion | flops 439877632 | bytes 8200832 | tf_op jit(solution)/shard_map/while/body/eval_jaxpr/gqtk,tgqd->kgd/dot_general | solution.py:71
  72.2 0.9 copy-done.10
  73.1 1.2 constant_dynamic-slice_fusion.9
  74.4 4.6 %fusion.75 = (f32[2,8,128]{2,1,0:T(8,128)S(1)}, f32[2,8,128,832]{2,3,1,0:T(8,128)}) fusion(pred[128,832]{0,1:T(8,128)(4,1)S(1)} %dynamic-slice_bitcast_fusion.2, bf16[1,128,2,8,128]{4,3,2,1,0:T(8,128)(2,1)S(1)} %constant_dynamic-slice_fusion.9, bf16[768,2,128]{2,0,1:T(8,128)(2,1)S(1)} %bitcast.182, bf16[64,2,128]{2,0,1:T(8,128)(2,1)S(1)} %get-tuple-element.380), kind=kOutput, calls=%fused_computation.85.clone.1 | convolution fusion | flops 445580096 | bytes 7880704 | tf_op jit(solution)/shard_map/while/body/eval_jaxpr/sub | solution.py:52
  79.1 1.2 constant_dynamic-slice_fusion.11
  80.4 7.1 %fusion.77 = (f32[2,8,128]{2,1,0:T(8,128)S(1)}, f32[2,832,128,8]{2,1,3,0:T(8,128)}) fusion(f32[2,8,128,832]{2,3,1,0:T(8,128)} %get-tuple-element.336, f32[2,8,128]{2,1,0:T(8,128)S(1)} %get-tuple-element.337, bf16[1,128,2,8,128]{4,3,2,1,0:T(8,128)(2,1)S(1)} %constant_dynamic-slice_fusion.11, pred[128]{0:T(512)(128)(4,1)S(1)} %fusion.76, ...), kind=kOutput, calls=%fused_computation.7.clone.1 | convolution fusion | flops 442431488 | bytes 14598272 | tf_op jit(solution)/shard_map/while/body/eval_jaxpr/tgqd,kgd->gqtk/dot_general | solution.py:59
  87.6 4.2 %fusion.78 = bf16[2,8,128,832]{2,3,1,0:T(8,128)(2,1)S(1)} fusion(f32[2,832,128,8]{2,1,3,0:T(8,128)} %get-tuple-element.338, f32[2,8,128]{2,1,0:T(8,128)S(1)} %get-tuple-element.339, f32[2,8,128,832]{2,3,1,0:T(8,128)S(1)} %bitcast.181, f32[2,8,128]{2,1,0:T(8,128)S(1)} %get-tuple-element.337), kind=kLoop, calls=%fused_computation.9.clone.1 | loop fusion | flops 6815744 | bytes 17055744 | tf_op jit(solution)/shard_map/while/body/eval_jaxpr/convert_element_type | solution.py:63
  91.8 1.6 fusion.79
  93.4 2.2 %copy.203 = bf16[1,128,2,8,128]{4,3,2,1,0:T(8,128)(2,1)} copy(bf16[1,128,2,8,128]{1,4,3,2,0:T(8,128)(2,1)} %fusion.79) | data formatting | bytes 1048576 | tf_op jit(solution)/shard_map/while/body/jit(dynamic_update_index_in_dim)/dynamic_update_slice | solution.py:115
  95.6 4.7 %fusion.80 = bf16[1,128,2,8,128]{1,4,3,2,0:T(8,128)(2,1)} fusion(pred[128]{0:T(512)(128)(4,1)S(1)} %fusion.76, bf16[768,2,128]{2,0,1:T(8,128)(2,1)} %bitcast.185, bf16[64,2,128]{2,0,1:T(8,128)(2,1)S(1)} %get-tuple-element.377, f32[2,8,128,832]{2,3,1,0:T(8,128)} %get-tuple-element.336, f32[2,8,128]{2,1,0:T(8,128)S(1)} %get-tuple-element.337), kind=kOutput, calls=%fused_computation.31.clone.1 | convolution fusion | flops 440991744 | bytes 7774336 | tf_op jit(solution)/shard_map/while/body/eval_jaxpr/gqtk,kgd->tgqd/dot_general | solution.py:56
  100.3 2.3 %copy.204 = bf16[1,128,2,8,128]{4,3,2,1,0:T(8,128)(2,1)} copy(bf16[1,128,2,8,128]{1,4,3,2,0:T(8,128)(2,1)} %fusion.80) | data formatting | bytes 1048576 | tf_op jit(solution)/shard_map/while/body/jit(dynamic_update_index_in_dim)/dynamic_update_slice | solution.py:115
  102.6 2.4 %constant_dynamic-update-slice_fusion.3 = (bf16[2,128,2,8,128]{4,3,2,1,0:T(8,128)(2,1)}, bf16[2,128,2,8,128]{4,3,2,1,0:T(8,128)(2,1)}) fusion(bf16[2,128,2,8,128]{4,3,2,1,0:T(8,128)(2,1)} %get-tuple-element.358, bf16[1,128,2,8,128]{4,3,2,1,0:T(8,128)(2,1)} %copy.203, s32[]{:T(128)} %get-tuple-element.356, ...), kind=kLoop, calls=%fused_computation.42.clone.1 | loop fusion | bytes 2097664 | tf_op jit(solution)/shard_map/while/body/jit(dynamic_update_index_in_dim)/dynamic_update_slice | solution.py:115
  105.0 3.0 %fusion.81 = f32[2,832,2,128]{3,1,2,0:T(8,128)} fusion(f32[2,832,2,128]{3,1,2,0:T(8,128)} %get-tuple-element.359, s32[]{:T(128)} %get-tuple-element.356, bf16[2,8,128,832]{2,3,1,0:T(8,128)(2,1)S(1)} %fusion.78, bf16[1,128,2,8,128]{4,3,2,1,0:T(8,128)(2,1)} %copy-done), kind=kOutput, calls=%fused_computation.28.clone.1 | convolution fusion | flops 436420608 | bytes 4784640 | tf_op jit(solution)/shard_map/while/body/eval_jaxpr/gqtk,tgqd->kgd/dot_general | solution.py:68
  108.0 5.1 %fusion.82 = f32[2,832,2,128]{3,1,2,0:T(8,128)} fusion(f32[2,832,2,128]{3,1,2,0:T(8,128)} %get-tuple-element.360, s32[]{:T(128)} %get-tuple-element.356, bf16[1,128,2,8,128]{4,3,2,1,0:T(8,128)(2,1)S(1)} %copy-done.4, pred[128]{0:T(512)(128)(4,1)S(1)} %fusion.76, f32[2,8,128,832]{2,3,1,0:T(8,128)} %get-tuple-element.336, ...), kind=kOutput, calls=%fused_computation.24.clone.1 | convolution fusion | flops 439877632 | bytes 8200832 | tf_op jit(solution)/shard_map/while/body/eval_jaxpr/gqtk,tgqd->kgd/dot_general | solution.py:71
  113.1 1.6 slice_reduce_fusion
  114.7 1.5 slice_reduce_fusion.1
  116.3 1.6 copy.145
  118.0 1.3 copy.146
  119.4 3.1 %scatter_fusion.1 = f32[8,128,2,128]{3,1,2,0:T(8,128)S(1)} fusion(f32[8,128,2,128]{3,1,2,0:T(8,128)S(1)} %broadcast.244.clone.1, s32[12]{0:T(128)S(1)} %reshape.299, f32[12,128,2,128]{3,1,2,0:T(8,128)} %copy.146), kind=kCustom, calls=%fused_computation.3 | custom fusion | flops 393216 | bytes 4718640 | tf_op jit(solution)/shard_map/scatter-add | solution.py:130
  122.6 1.0 copy-done.6
  123.6 1.6 copy.142
  125.5 1.8 scatter_fusion
  127.4 1.0 copy-done.5
  128.4 20.4 %all-reduce.4.cloned.1.call-done = (f32[64,2,128]{2,0,1:T(8,128)}, f32[64,2,128]{2,0,1:T(8,128)}) async-done(((f32[64,2,128]{2,0,1:T(8,128)}, f32[64,2,128]{2,0,1:T(8,128)}), (f32[64,2,128]{2,0,1:T(8,128)}, f32[64,2,128]{2,0,1:T(8,128)})) %all-reduce.4.cloned.1.call-update) | async-done | bytes 131088 | tf_op jit(solution)/shard_map/psum | solution.py:136
  148.8 1.5 copy.150
  150.3 1.5 copy.151
  151.8 24.6 %reduce-scatter.5.cloned.1.call-done = f32[2,128,2,128]{3,1,2,0:T(8,128)} async-done(((f32[8,128,2,128]{3,1,2,0:T(8,128)}), f32[2,128,2,128]{3,1,2,0:T(8,128)}) %reduce-scatter.5.cloned.1.call-update) | async-done | bytes 262160 | tf_op jit(solution)/shard_map/reduce_scatter | solution.py:134
  176.4 1.0 convert_element_type.32
  178.2 25.6 %reduce-scatter.3.cloned.1.call-done = f32[2,128,2,128]{3,1,2,0:T(8,128)} async-done(((f32[8,128,2,128]{3,1,2,0:T(8,128)}), f32[2,128,2,128]{3,1,2,0:T(8,128)}) %reduce-scatter.3.cloned.1.call-update) | async-done | bytes 262160 | tf_op jit(solution)/shard_map/reduce_scatter | solution.py:133
  203.8 1.0 convert_element_type.30
  (123 shorter events, 7.2 us)
Async XLA Ops:
  7.2 141.6 %all-reduce.4.cloned.1.call-start = ((), (), s32[]{:S(2)}) async-start(), calls=%async_computation.4 | async-start | bytes 262144 | tf_op jit(solution)/shard_map/psum | solution.py:136
  11.7 18.4 %copy-start.14 = (bf16[64,2,128]{2,1,0:T(2,128)(2,1)S(1)}, bf16[64,2,128]{2,1,0:T(2,128)(2,1)}, u32[]{:S(2)}) copy-start(bf16[64,2,128]{2,1,0:T(2,128)(2,1)} %param.17) | copy-start | bytes 98308
  11.7 18.4 %copy-start.15 = (bf16[64,2,128]{2,1,0:T(2,128)(2,1)S(1)}, bf16[64,2,128]{2,1,0:T(2,128)(2,1)}, u32[]{:S(2)}) copy-start(bf16[64,2,128]{2,1,0:T(2,128)(2,1)} %param.16) | copy-start | bytes 98308
  31.2 0.9 copy-start.10
  31.2 6.8 %copy-start.12 = (pred[2,128,832]{1,2,0:T(8,128)(4,1)}, pred[2,128,832]{1,2,0:T(8,128)(4,1)S(1)}, u32[]{:S(2)}) copy-start(pred[2,128,832]{1,2,0:T(8,128)(4,1)S(1)} %get-tuple-element.378) | copy-start | bytes 638980 | tf_op jit(solution)/shard_map/while
  31.2 6.9 %copy-start.8 = (bf16[2,6,128,2,128]{4,2,3,1,0:T(8,128)(2,1)}, bf16[2,6,128,2,128]{4,2,3,1,0:T(8,128)(2,1)S(1)}, u32[]{:S(2)}) copy-start(bf16[2,6,128,2,128]{4,2,3,1,0:T(8,128)(2,1)S(1)} %get-tuple-element.376) | copy-start | bytes 2359300 | tf_op jit(solution)/shard_map/while
  32.1 5.9 %copy-start.1 = (bf16[1,6,128,2,128]{4,2,1,3,0:T(8,128)(2,1)}, bf16[1,6,128,2,128]{4,2,1,3,0:T(8,128)(2,1)S(1)}, u32[]{:S(2)}) copy-start(bf16[1,6,128,2,128]{4,2,1,3,0:T(8,128)(2,1)S(1)} %copy.201) | copy-start | bytes 1179652 | tf_op jit(solution)/shard_map/while
  33.4 4.7 %copy-start = (bf16[1,128,2,8,128]{4,3,2,1,0:T(8,128)(2,1)}, bf16[1,128,2,8,128]{4,3,2,1,0:T(8,128)(2,1)S(1)}, u32[]{:S(2)}) copy-start(bf16[1,128,2,8,128]{4,3,2,1,0:T(8,128)(2,1)S(1)} %constant_dynamic-slice_fusion.9) | copy-start | bytes 1572868 | tf_op jit(solution)/shard_map/while
  38.1 8.4 %copy-start.7 = (bf16[1,6,128,2,128]{4,2,1,3,0:T(8,128)(2,1)}, bf16[1,6,128,2,128]{4,2,1,3,0:T(8,128)(2,1)S(1)}, u32[]{:S(2)}) copy-start(bf16[1,6,128,2,128]{4,2,1,3,0:T(8,128)(2,1)S(1)} %copy.202) | copy-start | bytes 1179652 | tf_op jit(solution)/shard_map/while
  39.4 7.2 %copy-start.3 = (bf16[1,128,2,8,128]{4,3,2,1,0:T(8,128)(2,1)}, bf16[1,128,2,8,128]{4,3,2,1,0:T(8,128)(2,1)S(1)}, u32[]{:S(2)}) copy-start(bf16[1,128,2,8,128]{4,3,2,1,0:T(8,128)(2,1)S(1)} %constant_dynamic-slice_fusion.11) | copy-start | bytes 1572868 | tf_op jit(solution)/shard_map/while
  39.4 7.2 %slice-start = ((s8[6815744]{0:T(1024)(128)(4,1)}), s8[4194304]{0:T(1024)(128)(4,1)S(1)}, s32[]{:S(2)}) async-start(s8[6815744]{0:T(1024)(128)(4,1)} %bitcast.180), calls=%async_computation.5 | async-start | bytes 8388608 | tf_op jit(solution)/shard_map/while
  39.4 7.2 %slice-start.1 = ((s8[6815744]{0:T(1024)(128)(4,1)}), s8[2621440]{0:T(1024)(128)(4,1)S(1)}, s32[]{:S(2)}) async-start(s8[6815744]{0:T(1024)(128)(4,1)} %bitcast.180), calls=%async_computation.6 | async-start | bytes 5242880 | tf_op jit(solution)/shard_map/while
  46.6 4.2 %copy-start.2 = (bf16[1,6,128,2,128]{4,2,1,3,0:T(8,128)(2,1)S(1)}, bf16[1,6,128,2,128]{4,2,1,3,0:T(8,128)(2,1)}, u32[]{:S(2)}) copy-start(bf16[1,6,128,2,128]{4,2,1,3,0:T(8,128)(2,1)} %copy-done.1) | copy-start | bytes 1179652 | tf_op jit(solution)/shard_map/while
  61.6 5.4 %copy-start.4 = (bf16[1,128,2,8,128]{4,3,2,1,0:T(8,128)(2,1)S(1)}, bf16[1,128,2,8,128]{4,3,2,1,0:T(8,128)(2,1)}, u32[]{:S(2)}) copy-start(bf16[1,128,2,8,128]{4,3,2,1,0:T(8,128)(2,1)} %copy-done.3) | copy-start | bytes 1572868 | tf_op jit(solution)/shard_map/while
  67.0 5.1 %copy-start.9 = (bf16[2,6,128,2,128]{4,2,3,1,0:T(8,128)(2,1)S(1)}, bf16[2,6,128,2,128]{4,2,3,1,0:T(8,128)(2,1)}, u32[]{:S(2)}) copy-start(bf16[2,6,128,2,128]{4,2,3,1,0:T(8,128)(2,1)} %copy-done.8) | copy-start | bytes 2359300 | tf_op jit(solution)/shard_map/while
  67.0 5.1 %copy-start.11 = (bf16[2,6,128,2,128]{4,2,3,1,0:T(8,128)(2,1)S(1)}, bf16[2,6,128,2,128]{4,2,3,1,0:T(8,128)(2,1)}, u32[]{:S(2)}) copy-start(bf16[2,6,128,2,128]{4,2,3,1,0:T(8,128)(2,1)} %copy-done.10) | copy-start | bytes 2359300 | tf_op jit(solution)/shard_map/while
  67.0 5.1 %copy-start.13 = (pred[2,128,832]{1,2,0:T(8,128)(4,1)S(1)}, pred[2,128,832]{1,2,0:T(8,128)(4,1)}, u32[]{:S(2)}) copy-start(pred[2,128,832]{1,2,0:T(8,128)(4,1)} %copy-done.12) | copy-start | bytes 638980 | tf_op jit(solution)/shard_map/while
  72.2 0.9 copy-start.10
  72.2 6.8 %copy-start.12 = (pred[2,128,832]{1,2,0:T(8,128)(4,1)}, pred[2,128,832]{1,2,0:T(8,128)(4,1)S(1)}, u32[]{:S(2)}) copy-start(pred[2,128,832]{1,2,0:T(8,128)(4,1)S(1)} %get-tuple-element.378) | copy-start | bytes 638980 | tf_op jit(solution)/shard_map/while
  72.2 6.9 %copy-start.8 = (bf16[2,6,128,2,128]{4,2,3,1,0:T(8,128)(2,1)}, bf16[2,6,128,2,128]{4,2,3,1,0:T(8,128)(2,1)S(1)}, u32[]{:S(2)}) copy-start(bf16[2,6,128,2,128]{4,2,3,1,0:T(8,128)(2,1)S(1)} %get-tuple-element.376) | copy-start | bytes 2359300 | tf_op jit(solution)/shard_map/while
  73.1 5.9 %copy-start.1 = (bf16[1,6,128,2,128]{4,2,1,3,0:T(8,128)(2,1)}, bf16[1,6,128,2,128]{4,2,1,3,0:T(8,128)(2,1)S(1)}, u32[]{:S(2)}) copy-start(bf16[1,6,128,2,128]{4,2,1,3,0:T(8,128)(2,1)S(1)} %copy.201) | copy-start | bytes 1179652 | tf_op jit(solution)/shard_map/while
  74.4 4.7 %copy-start = (bf16[1,128,2,8,128]{4,3,2,1,0:T(8,128)(2,1)}, bf16[1,128,2,8,128]{4,3,2,1,0:T(8,128)(2,1)S(1)}, u32[]{:S(2)}) copy-start(bf16[1,128,2,8,128]{4,3,2,1,0:T(8,128)(2,1)S(1)} %constant_dynamic-slice_fusion.9) | copy-start | bytes 1572868 | tf_op jit(solution)/shard_map/while
  79.1 8.4 %copy-start.7 = (bf16[1,6,128,2,128]{4,2,1,3,0:T(8,128)(2,1)}, bf16[1,6,128,2,128]{4,2,1,3,0:T(8,128)(2,1)S(1)}, u32[]{:S(2)}) copy-start(bf16[1,6,128,2,128]{4,2,1,3,0:T(8,128)(2,1)S(1)} %copy.202) | copy-start | bytes 1179652 | tf_op jit(solution)/shard_map/while
  80.4 7.2 %copy-start.3 = (bf16[1,128,2,8,128]{4,3,2,1,0:T(8,128)(2,1)}, bf16[1,128,2,8,128]{4,3,2,1,0:T(8,128)(2,1)S(1)}, u32[]{:S(2)}) copy-start(bf16[1,128,2,8,128]{4,3,2,1,0:T(8,128)(2,1)S(1)} %constant_dynamic-slice_fusion.11) | copy-start | bytes 1572868 | tf_op jit(solution)/shard_map/while
  80.4 7.2 %slice-start = ((s8[6815744]{0:T(1024)(128)(4,1)}), s8[4194304]{0:T(1024)(128)(4,1)S(1)}, s32[]{:S(2)}) async-start(s8[6815744]{0:T(1024)(128)(4,1)} %bitcast.180), calls=%async_computation.5 | async-start | bytes 8388608 | tf_op jit(solution)/shard_map/while
  80.4 7.2 %slice-start.1 = ((s8[6815744]{0:T(1024)(128)(4,1)}), s8[2621440]{0:T(1024)(128)(4,1)S(1)}, s32[]{:S(2)}) async-start(s8[6815744]{0:T(1024)(128)(4,1)} %bitcast.180), calls=%async_computation.6 | async-start | bytes 5242880 | tf_op jit(solution)/shard_map/while
  87.6 4.2 %copy-start.2 = (bf16[1,6,128,2,128]{4,2,1,3,0:T(8,128)(2,1)S(1)}, bf16[1,6,128,2,128]{4,2,1,3,0:T(8,128)(2,1)}, u32[]{:S(2)}) copy-start(bf16[1,6,128,2,128]{4,2,1,3,0:T(8,128)(2,1)} %copy-done.1) | copy-start | bytes 1179652 | tf_op jit(solution)/shard_map/while
  102.6 5.4 %copy-start.4 = (bf16[1,128,2,8,128]{4,3,2,1,0:T(8,128)(2,1)S(1)}, bf16[1,128,2,8,128]{4,3,2,1,0:T(8,128)(2,1)}, u32[]{:S(2)}) copy-start(bf16[1,128,2,8,128]{4,3,2,1,0:T(8,128)(2,1)} %copy-done.3) | copy-start | bytes 1572868 | tf_op jit(solution)/shard_map/while
  108.0 5.1 %copy-start.9 = (bf16[2,6,128,2,128]{4,2,3,1,0:T(8,128)(2,1)S(1)}, bf16[2,6,128,2,128]{4,2,3,1,0:T(8,128)(2,1)}, u32[]{:S(2)}) copy-start(bf16[2,6,128,2,128]{4,2,3,1,0:T(8,128)(2,1)} %copy-done.8) | copy-start | bytes 2359300 | tf_op jit(solution)/shard_map/while
  108.0 5.1 %copy-start.11 = (bf16[2,6,128,2,128]{4,2,3,1,0:T(8,128)(2,1)S(1)}, bf16[2,6,128,2,128]{4,2,3,1,0:T(8,128)(2,1)}, u32[]{:S(2)}) copy-start(bf16[2,6,128,2,128]{4,2,3,1,0:T(8,128)(2,1)} %copy-done.10) | copy-start | bytes 2359300 | tf_op jit(solution)/shard_map/while
  108.0 5.1 %copy-start.13 = (pred[2,128,832]{1,2,0:T(8,128)(4,1)S(1)}, pred[2,128,832]{1,2,0:T(8,128)(4,1)}, u32[]{:S(2)}) copy-start(pred[2,128,832]{1,2,0:T(8,128)(4,1)} %copy-done.12) | copy-start | bytes 638980 | tf_op jit(solution)/shard_map/while
  116.3 60.1 %reduce-scatter.5.cloned.1.call-start = ((), (), s32[]{:S(2)}) async-start(), calls=%async_computation.3 | async-start | bytes 1310720 | tf_op jit(solution)/shard_map/reduce_scatter | solution.py:134
  117.9 1.4 copy-start.16
  122.6 1.0 copy-start.6
  123.6 80.3 %reduce-scatter.3.cloned.1.call-start = ((), (), s32[]{:S(2)}) async-start(), calls=%async_computation.2 | async-start | bytes 1310720 | tf_op jit(solution)/shard_map/reduce_scatter | solution.py:133
  127.4 1.0 copy-start.5
Sparse Core Ops, SparseCore 0:
  116.4 32.3 all-reduce.3
  151.5 24.8 reduce-scatter.4
  178.9 24.8 reduce-scatter.2
where the time goes:
time: 213 us; the launch traced here: 212 us
  waiting for transfers between devices  70.6 us (33%)
  matrix products  52.3 us (25%)
  local copies, waits for them, and re-layouts  36.9 us (17%)
  other arithmetic  21.3 us (10%)
  blocking collectives  15.9 us (7%)
  between operations  14.7 us (7%)
    reduce_scatter x1, waiting for transfers between devices, on_device(): lax.psum_scatter(full_keys, 'seq', scatter_dimension=0, tiled=True)  25.6 us
    reduce_scatter x1, waiting for transfers between devices, on_device(): lax.psum_scatter(full_values, 'seq', scatter_dimension=0, tiled=True)  24.6 us
    psum x1, waiting for transfers between devices, on_device(): prefix_keys_all, prefix_values_all = lax.psum((prefix_gk, prefix_gv), 'seq')  20.4 us
    dot_general x2, matrix products, attend(): jnp.einsum('tgqd,kgd->gqtk', masked_grad, value_rows, preferred_element_t...  14.3 us
    dynamic_update_slice x6, local copies, waits for them, and re-layouts, on_device(): lax.map(one_block, (query_tiles, grad_tiles, listed_keys, listed_values,...  13.9 us
    dot_general x2, matrix products, attend(): jnp.einsum('gqtk,tgqd->kgd', prob_bf, masked_grad, preferred_element_type...  10.2 us
    dot_general x2, matrix products, attend(): jnp.einsum('gqtk,kgd->tgqd', prob_bf, value_rows, preferred_element_type=...  9.39 us
    sub x2, matrix products, attend(): weights = jnp.where(visible[None, None], jnp.exp(scores - maxima), 0.0)  9.22 us
  transfers between devices with their start and end apart: 3, of which 3 were waited for; matrix products, arithmetic and copies ran while one was open for 7% of the time, Pallas kernels for 0%

commit v1 on v0

v1 whole, which is shorter than its diff:
```python
import functools
import math

import jax
import jax.numpy as jnp
from jax import lax
from jax.experimental import pallas as pl
from jax.experimental.pallas import tpu as pltpu
from jax.sharding import PartitionSpec as P

BLK = 128
LANES = 256
masked_score = -1e30


def dot(a, b, ca, cb):
    return lax.dot_general(a, b, (((ca,), (cb,)), ((), ())), preferred_element_type=jnp.float32)


def attend_kernel(
    per_dev, blocks, gids, owner, offset, length, q_ref, do_ref, kv_ref, pk_ref, pv_ref,
    o_ref, dq_ref, gkv_ref, gp_ref, k_s, v_s, p_s, ds_s, acc,
):
    b = pl.program_id(0)
    g = pl.program_id(1)
    last = (b == pl.num_programs(0) - 1) & (g == pl.num_programs(1) - 1)
    psz = pk_ref.shape[1]
    qheads, width = q_ref.shape[2], q_ref.shape[3]
    rows = BLK * qheads
    scaling = 1.0 / math.sqrt(width)
    i = lax.axis_index("seq") * per_dev + b
    doc = length[0]

    entries = [i - 1, i]
    entries += [gids[j] for j in range(gids.shape[0])]
    entries += [owner[b, j] * per_dev + offset[b, j] for j in range(owner.shape[1])]
    places, limits = [], []
    for j, e in enumerate(entries):
        ok = (e >= 0) & (e <= i)
        for earlier in entries[:j]:
            ok = ok & (e != earlier)
        places.append(jnp.where(ok, e, i))
        limits.append(jnp.where(ok, doc - e * BLK, 0))

    @pl.when((b == 0) & (g == 0))
    def _():
        acc[...] = jnp.zeros_like(acc)
        gp_ref[...] = jnp.zeros_like(gp_ref)

    k_s[0:psz, :] = pk_ref[g]
    v_s[0:psz, :] = pv_ref[g]
    for j, e in enumerate(places):
        at = pl.ds(psz + j * BLK, BLK)
        dev = e // per_dev
        inner = pl.ds(pl.multiple_of((e - dev * per_dev) * BLK, BLK), BLK)
        k_s[at, :] = kv_ref[dev, 0, g, inner, :]
        v_s[at, :] = kv_ref[dev, 1, g, inner, :]

    keys = k_s[...]
    values = v_s[...]
    keys_t = keys.T
    values_t = values.T
    step = LANES // qheads
    for c in range(rows // LANES):
        q = q_ref[c * step : (c + 1) * step, 0].reshape(LANES, width)
        row_t = i * BLK + c * step + lax.broadcasted_iota(jnp.int32, (LANES, width), 0) // qheads
        do = do_ref[c * step : (c + 1) * step, 0].reshape(LANES, width)
        do = jnp.where(row_t < doc, do.astype(jnp.float32), 0.0).astype(jnp.bfloat16)
        s = dot(keys, q, 1, 1) * (scaling * math.log2(math.e))
        key_at = lax.broadcasted_iota(jnp.int32, (BLK, LANES), 0)
        lane_t = c * step + lax.broadcasted_iota(jnp.int32, (BLK, LANES), 1) // qheads
        parts = [s[0:psz]]
        for j in range(len(places)):
            visible = key_at < limits[j]
            if j == 1:
                visible = visible & (key_at <= lane_t)
            parts.append(jnp.where(visible, s[psz + j * BLK : psz + (j + 1) * BLK], masked_score))
        s = jnp.concatenate(parts, axis=0)
        w = jnp.exp2(s - jnp.max(s, axis=0, keepdims=True))
        p = w * (1.0 / jnp.sum(w, axis=0, keepdims=True))
        p_bf = p.astype(jnp.bfloat16)
        p_s[:, c * LANES : (c + 1) * LANES] = p_bf
        dp = dot(values, do, 1, 1)
        delta = jnp.sum(p * dp, axis=0, keepdims=True)
        ds = (p * (dp - delta)).astype(jnp.bfloat16)
        ds_s[:, c * LANES : (c + 1) * LANES] = ds
        o = dot(values_t, p_bf, 1, 0).T
        o = jnp.where(row_t < doc, o, 0.0).astype(jnp.bfloat16)
        o_ref[c * step : (c + 1) * step, 0] = o.reshape(step, qheads, width)
        dq = (dot(keys_t, ds, 1, 0) * scaling).T.astype(jnp.bfloat16)
        dq_ref[c * step : (c + 1) * step, 0] = dq.reshape(step, qheads, width)

    all_t = i * BLK + lax.broadcasted_iota(jnp.int32, (rows, width), 0) // qheads
    do = do_ref[:, 0].reshape(rows, width)
    do = jnp.where(all_t < doc, do.astype(jnp.float32), 0.0).astype(jnp.bfloat16)
    gk = dot(ds_s[...], q_ref[:, 0].reshape(rows, width), 1, 0) * scaling
    gv = dot(p_s[...], do, 1, 0)
    for which, grad in ((0, gk), (1, gv)):
        gp_ref[which, g] += grad[0:psz]
        for j, e in enumerate(places):
            dev = e // per_dev
            inner = pl.ds(pl.multiple_of((e - dev * per_dev) * BLK, BLK), BLK)
            acc[dev, which, g, inner, :] += grad[psz + j * BLK : psz + (j + 1) * BLK]

    @pl.when(last)
    def _():
        gkv_ref[...] = acc[...].astype(gkv_ref.dtype)


def attend(q, do, kv, pk, pv, gids, owner, offset, length):
    tokens, groups, qheads, width = q.shape
    devices, per_tok = kv.shape[0], kv.shape[3]
    per_dev = tokens // BLK
    psz = pk.shape[1]
    total = psz + BLK * (2 + gids.shape[0] + owner.shape[1])
    tile = pl.BlockSpec((BLK, 1, qheads, width), lambda b, g: (b, g, 0, 0))
    smem = pl.BlockSpec(memory_space=pltpu.SMEM)
    vmem = pl.BlockSpec(memory_space=pltpu.VMEM)
    return pl.pallas_call(
        functools.partial(attend_kernel, per_dev, devices * per_dev),
        grid=(per_dev, groups),
        in_specs=[smem] * 4 + [tile, tile] + [vmem] * 3,
        out_specs=[tile, tile, vmem, vmem],
        out_shape=[
            jax.ShapeDtypeStruct(q.shape, jnp.bfloat16),
            jax.ShapeDtypeStruct(q.shape, jnp.bfloat16),
            jax.ShapeDtypeStruct(kv.shape, jnp.bfloat16),
            jax.ShapeDtypeStruct((2, groups, psz, width), jnp.float32),
        ],
        scratch_shapes=[
            pltpu.VMEM((total, width), jnp.bfloat16),
            pltpu.VMEM((total, width), jnp.bfloat16),
            pltpu.VMEM((total, BLK * qheads), jnp.bfloat16),
            pltpu.VMEM((total, BLK * qheads), jnp.bfloat16),
            pltpu.VMEM(kv.shape, jnp.float32),
        ],
        compiler_params=pltpu.CompilerParams(
            vmem_limit_bytes=50 * 2**20, dimension_semantics=("arbitrary", "arbitrary")
        ),
        cost_estimate=pl.CostEstimate(
            flops=10 * tokens * groups * qheads * total * width,
            bytes_accessed=8 * tokens * groups * qheads * width,
            transcendentals=tokens * groups * qheads * total,
        ),
    )(gids, owner, offset, length, q, do, kv, pk, pv)


def on_device(
    queries, seq_keys, seq_values, out_grad, prefix_keys, prefix_values,
    global_ids, rand_owner, rand_offset, doc_length,
):
    tokens, groups, width = seq_keys.shape
    shape = (tokens, groups, queries.shape[1] // groups, width)
    own = jnp.stack([seq_keys, seq_values]).transpose(0, 2, 1, 3)
    kv = lax.all_gather(own, "seq", axis=0)
    o, dq, gkv, gp = attend(
        queries.reshape(shape), out_grad.reshape(shape), kv,
        prefix_keys.transpose(1, 0, 2), prefix_values.transpose(1, 0, 2),
        global_ids, rand_owner, rand_offset, doc_length,
    )
    mine = lax.psum_scatter(gkv, "seq", scatter_dimension=0)
    gp = lax.psum(gp, "seq")
    mine = mine.astype(jnp.bfloat16).transpose(0, 2, 1, 3)
    gp = gp.transpose(0, 2, 1, 3)
    return (o.reshape(queries.shape), dq.reshape(queries.shape), mine[0], mine[1], gp[0], gp[1])


def solution(mesh):
    tok = P(("groups", "seq"), "head", None)
    pre = P(None, "head", None)
    row = P(("groups", "seq"), None)
    out = P("groups", "head", None)
    return jax.shard_map(
        on_device,
        mesh=mesh,
        in_specs=(tok, tok, tok, tok, pre, pre, P("groups"), row, row, P("groups")),
        out_specs=(tok, tok, tok, tok, out, out),
        check_vma=False,
    )
```

time: 213 us -> 122 us (0.57)
  matrix products: 52.3 us -> 0 us
  local copies, waits for them, and re-layouts: 36.9 us -> 7.86 us
  Pallas kernels: 0 us -> 21.6 us
  other arithmetic: 21.3 us -> 0.73 us
  blocking collectives: 15.9 us -> 0 us
  waiting for transfers between devices: 70.6 us -> 76.6 us
    dot_general x10 -> x0, matrix products: 43 us -> none  [the longest x2 14.3 us: attend(): jnp.einsum('tgqd,kgd->gqtk', masked_grad, value_rows, preferred_element_t...]
    reduce_scatter x2 -> x1, waiting for transfers between devices: 50.2 us -> 25.4 us  [on_device(): mine = lax.psum_scatter(gkv, 'seq', scatter_dimension=0)]
    pallas_call x0 -> x1, Pallas kernels: none -> 21.6 us  [attend(): pl.pallas_call(functools.partial(attend_kernel, per_dev, devices * per_de...]
    all_gather x0 -> x1, waiting for transfers between devices: none -> 19.8 us  [on_device(): kv = lax.all_gather(own, 'seq', axis=0)]
    all_gather x2 -> x0, blocking collectives: 15.9 us -> none  [the longest x1 8.62 us: on_device(): lax.all_gather(seq_values, 'seq', axis=0, tiled=True)]
    dynamic_update_slice x6 -> x0, local copies, waits for them, and re-layouts: 13.9 us -> none  [on_device(): lax.map(one_block, (query_tiles, grad_tiles, listed_keys, listed_values,...]
    psum x1, waiting for transfers between devices: 20.4 us -> 30.8 us  [on_device(): gp = lax.psum(gp, 'seq')]
    convert_element_type x4 -> x0, other arithmetic: 10.4 us -> none  [the longest x2 8.42 us: attend(): grad_score = (probability * (grad_prob - row_delta)).astype(jnp.bfloat16)]
  transfers between devices with their start and end apart: 3 -> 3, of which waited for: 3 -> 3; matrix products, arithmetic and copies ran while one was open for 7% -> 2% of each run, Pallas kernels for 0% -> 0%
where the time goes in v1:
time: 122 us; the launch traced here: 121 us
  waiting for transfers between devices  76.6 us (63%)
  Pallas kernels  21.6 us (18%)
  between operations  14.4 us (12%)
  local copies, waits for them, and re-layouts  7.86 us (6%)
    psum x1, waiting for transfers between devices, on_device(): gp = lax.psum(gp, 'seq')  30.8 us
    reduce_scatter x1, waiting for transfers between devices, on_device(): mine = lax.psum_scatter(gkv, 'seq', scatter_dimension=0)  25.4 us
    pallas_call x1, Pallas kernels, attend(): pl.pallas_call(functools.partial(attend_kernel, per_dev, devices * per_de...  21.6 us
    all_gather x1, waiting for transfers between devices, on_device(): kv = lax.all_gather(own, 'seq', axis=0)  19.8 us
    unnamed x18, local copies, waits for them, and re-layouts  4.9 us
  transfers between devices with their start and end apart: 3, of which 3 were waited for; matrix products, arithmetic and copies ran while one was open for 2% of the time, Pallas kernels for 0%

profile of v1, /device:TPU:0, one launch (start us, length us, event | category | flops | bytes accessed | tf_op | source)
XLA Modules:
  0.0 121.4 jit_solution(10255498814959277573)
XLA Ops:
  7.2 0.0 copy-start
  7.2 0.0 all-gather.3.cloned.1.call-start
  7.2 1.1 copy_bitcast_fusion
  8.3 0.7 maximum_bitcast_fusion
  9.0 0.0 copy-start.5
  9.0 0.0 copy-start.6
  9.0 0.0 all-gather.3.cloned.1.call-update
  9.1 0.0 all-reduce.2.cloned.1.call-start
  9.8 0.0 copy-done.5
  9.8 0.0 copy-done.6
  9.8 0.0 copy-start.3
  9.8 19.8 %all-gather.3.cloned.1.call-done = bf16[8,2,256,128]{3,2,1,0:T(8,128)(2,1)} async-done(((bf16[2,2,256,128]{3,2,1,0:T(8,128)(2,1)}), bf16[8,2,256,128]{3,2,1,0:T(8,128)(2,1)}) %all-gather.3.cloned.1.call-update) | async-done | bytes 1048592 | tf_op jit(solution)/shard_map/all_gather | solution.py:155
  29.6 0.0 copy-start.2
  29.6 0.0 copy-start.4
  29.6 0.0 copy-done
  29.6 0.0 copy-done.3
  29.6 0.7 copy-done.2
  30.3 0.0 copy-done.4
  30.3 0.0 copy-start.1
  30.3 1.2 %copy-done.1 = bf16[256,16,128]{2,1,0:T(8,128)(2,1)S(1)} copy-done((bf16[256,16,128]{2,1,0:T(8,128)(2,1)S(1)}, bf16[256,16,128]{2,1,0:T(8,128)(2,1)}, u32[]{:S(2)}) %copy-start.1) | copy-done | bytes 1048600
  31.5 21.6 %shard_map.145 = (bf16[256,2,8,128]{3,2,1,0:T(8,128)(2,1)}, bf16[256,2,8,128]{3,2,1,0:T(8,128)(2,1)}, bf16[4,2,2,256,128]{4,3,2,1,0:T(8,128)(2,1)}, f32[2,2,64,128]{3,2,1,0:T(8,128)}) custom-call(s32[2]{0:T(128)S(1)} %copy-done.4, s32[2,2]{1,0:T(2,128)S(1)} %copy-done.2, s32[2,2]{1,0:T(2,128)S(1)} %copy-done.3, s32[1]{0:T(128)S(6)} %copy.36.length, ...), custom_call_target="tpu_custom_call" | custom-call | flops 4362076160 | bytes 4194304 | tf_op jit(solution)/shard_map/pallas_call | solution.py:119
  53.1 0.0 all-reduce.2.cloned.1.call-update
  53.1 0.0 reduce-scatter.2.cloned.1.call-start
  53.2 0.7 reduce-scatter.2.cloned.1.call-update
  53.9 30.8 %all-reduce.2.cloned.1.call-done = f32[2,64,2,128]{3,1,2,0:T(8,128)} async-done(((f32[2,64,2,128]{3,1,2,0:T(8,128)}), f32[2,64,2,128]{3,1,2,0:T(8,128)}) %all-reduce.2.cloned.1.call-update) | async-done | bytes 131088 | tf_op jit(solution)/shard_map/psum | solution.py:162
  84.7 0.9 slice_bitcast_fusion.2
  85.6 0.7 copy.30
  86.2 0.7 copy.29
  86.9 25.4 %reduce-scatter.2.cloned.1.call-done = bf16[1,2,2,256,128]{4,3,2,1,0:T(8,128)(2,1)} async-done(((bf16[4,2,2,256,128]{4,3,2,1,0:T(8,128)(2,1)}), bf16[1,2,2,256,128]{4,3,2,1,0:T(8,128)(2,1)}) %reduce-scatter.2.cloned.1.call-update) | async-done | bytes 262160 | tf_op jit(solution)/shard_map/reduce_scatter | solution.py:161
  112.3 1.0 slice_bitcast_fusion
  113.3 0.8 copy.28
  114.1 0.8 copy.27
  (1 shorter events, 0.0 us)
Async XLA Ops:
  7.2 22.4 %copy-start = (bf16[256,16,128]{2,1,0:T(8,128)(2,1)S(1)}, bf16[256,16,128]{2,1,0:T(8,128)(2,1)}, u32[]{:S(2)}) copy-start(bf16[256,16,128]{2,1,0:T(8,128)(2,1)} %param.10) | copy-start | bytes 3145732
  7.2 22.4 %all-gather.3.cloned.1.call-start = ((), (), s32[]{:S(2)}) async-start(), calls=%async_computation.3 | async-start | bytes 1310720 | tf_op jit(solution)/shard_map/all_gather | solution.py:155
  9.0 0.8 copy-start.5
  9.0 0.8 copy-start.6
  9.1 75.6 %all-reduce.2.cloned.1.call-start = ((), (), s32[]{:S(2)}) async-start(), calls=%async_computation.2 | async-start | bytes 262144 | tf_op jit(solution)/shard_map/psum | solution.py:162
  9.8 19.8 %copy-start.3 = (s32[2,2]{1,0:T(2,128)S(1)}, s32[2,2]{1,0:T(2,128)}, u32[]{:S(2)}) copy-start(s32[2,2]{1,0:T(2,128)} %offset.1) | copy-start | bytes 52
  29.6 0.7 copy-start.2
  29.6 0.7 copy-start.4
  30.3 1.2 %copy-start.1 = (bf16[256,16,128]{2,1,0:T(8,128)(2,1)S(1)}, bf16[256,16,128]{2,1,0:T(8,128)(2,1)}, u32[]{:S(2)}) copy-start(bf16[256,16,128]{2,1,0:T(8,128)(2,1)} %param.13) | copy-start | bytes 3145732
  53.1 59.1 %reduce-scatter.2.cloned.1.call-start = ((), (), s32[]{:S(2)}) async-start(), calls=%async_computation.1 | async-start | bytes 1310720 | tf_op jit(solution)/shard_map/reduce_scatter | solution.py:161
Sparse Core Ops, SparseCore 0:
  10.1 19.4 all-gather.2
  53.3 31.3 all-reduce.1
  87.4 24.8 reduce-scatter.1

commit v2 on v1

--- a/solution.py
+++ b/solution.py
@@ -10,6 +10,7 @@
 
 BLK = 128
 LANES = 256
+MESH = pl.DeviceIdType.MESH
 masked_score = -1e30
 
 
@@ -145,6 +146,211 @@
     )(gids, owner, offset, length, q, do, kv, pk, pv)
 
 
+def greet(n, me):
+    barrier = pltpu.get_barrier_semaphore()
+    for step in range(1, n):
+        pl.semaphore_signal(
+            barrier, inc=1, device_id={"seq": lax.rem(me + step, n)}, device_id_type=MESH
+        )
+    pl.semaphore_wait(barrier, n - 1)
+
+
+def gather_kernel(n, own_ref, out_ref, send_sem, recv_sem):
+    me = lax.axis_index("seq")
+    chip, core = me // 2, me % 2
+    chips = n // 2
+    greet(n, me)
+
+    def push(src, origin, to, slot):
+        return pltpu.make_async_remote_copy(
+            src_ref=src, dst_ref=out_ref.at[origin], send_sem=send_sem.at[slot],
+            recv_sem=recv_sem.at[origin], device_id={"seq": to}, device_id_type=MESH,
+        )
+
+    for x in range(chips):
+        @pl.when(x > chip)
+        def _():
+            push(own_ref, me, x * 2 + core, x).start()
+
+    @pl.when(core == 0)
+    def _():
+        push(own_ref, me, me + 1, chips).start()
+
+    out_ref[me] = own_ref[...]
+    partner = chip * 2 + (1 - core)
+    for x in range(chips):
+        @pl.when(x < chip)
+        def _():
+            origin = x * 2 + core
+            push(own_ref, origin, partner, x).wait_recv()
+            push(out_ref.at[origin], origin, partner, x).start()
+
+    for x in range(chips):
+        @pl.when(x < chip)
+        def _():
+            push(own_ref, x * 2 + (1 - core), partner, x).wait_recv()
+            push(out_ref.at[x * 2 + core], x * 2 + core, partner, x).wait_send()
+
+        @pl.when(x > chip)
+        def _():
+            push(own_ref, me, x * 2 + core, x).wait_send()
+
+    @pl.when(core == 0)
+    def _():
+        push(own_ref, me, me + 1, chips).wait_send()
+
+    @pl.when(core == 1)
+    def _():
+        push(own_ref, me - 1, partner, chips).wait_recv()
+
+
+def gather(own, n):
+    vmem = pl.BlockSpec(memory_space=pltpu.VMEM)
+    return pl.pallas_call(
+        functools.partial(gather_kernel, n),
+        in_specs=[vmem],
+        out_specs=vmem,
+        out_shape=jax.ShapeDtypeStruct((n,) + own.shape, own.dtype),
+        scratch_shapes=[
+            pltpu.SemaphoreType.DMA((n // 2 + 1,)),
+            pltpu.SemaphoreType.DMA((n,)),
+        ],
+        compiler_params=pltpu.CompilerParams(
+            collective_id=0, has_side_effects=True, vmem_limit_bytes=24 * 2**20
+        ),
+    )(own)
+
+
+def reduce_kernel(
+    n, g_ref, p_ref, k_out, v_out, p_out, near, far, sums, p_near, p_sum, p_far,
+    near_send, near_recv, far_send, far_recv, p_send, p_recv, pf_send, pf_recv,
+):
+    me = lax.axis_index("seq")
+    chip, core = me // 2, me % 2
+    chips = n // 2
+    partner = chip * 2 + (1 - core)
+    greet(n, me)
+
+    def move(src, dst, ss, rs, to):
+        return pltpu.make_async_remote_copy(
+            src_ref=src, dst_ref=dst, send_sem=ss, recv_sem=rs,
+            device_id={"seq": to}, device_id_type=MESH,
+        )
+
+    def to_near(x):
+        return move(g_ref.at[x * 2 + (1 - core)], near.at[x], near_send.at[x], near_recv.at[x], partner)
+
+    def to_far(x):
+        return move(sums.at[x], far.at[chip], far_send.at[x], far_recv.at[chip], x * 2 + core)
+
+    def from_far(x):
+        return move(sums.at[x], far.at[x], far_send.at[x], far_recv.at[x], x * 2 + core)
+
+    def p_to_far(x):
+        return move(p_sum, p_far.at[chip], pf_send.at[x], pf_recv.at[chip], x * 2 + core)
+
+    def p_from_far(x):
+        return move(p_sum, p_far.at[x], pf_send.at[x], pf_recv.at[x], x * 2 + core)
+
+    p_first = move(p_ref.at[1 - core], p_near, p_send.at[0], p_recv.at[0], partner)
+    p_first.start()
+    for x in range(chips):
+        @pl.when(x < chip)
+        def _():
+            to_near(x).start()
+
+    @pl.when(core == 1)
+    def _():
+        to_near(chip).start()
+
+    for x in range(chips):
+        @pl.when(x < chip)
+        def _():
+            to_near(x).wait_recv()
+            total = g_ref[x * 2 + core].astype(jnp.float32) + near[x].astype(jnp.float32)
+            sums[x] = total.astype(sums.dtype)
+            to_far(x).start()
+
+    p_first.wait_recv()
+    p_sum[...] = p_ref[core] + p_near[...]
+    for x in range(chips):
+        @pl.when(x != chip)
+        def _():
+            p_to_far(x).start()
+    p_out[core] = p_sum[...]
+    for x in range(chips):
+        @pl.when(x != chip)
+        def _():
+            p_from_far(x).wait_recv()
+            p_out[core] += p_far[x]
+    p_mine = move(p_out.at[core], p_out.at[core], p_send.at[1], p_recv.at[1], partner)
+    p_theirs = move(p_out.at[core], p_out.at[1 - core], p_send.at[1], p_recv.at[1], partner)
+    p_mine.start()
+
+    @pl.when(core == 0)
+    def _():
+        to_near(chip).wait_recv()
+    for x in range(chips):
+        @pl.when(x > chip)
+        def _():
+            from_far(x).wait_recv()
+
+    for which, out in ((0, k_out), (1, v_out)):
+        mine = g_ref[me, which].astype(jnp.float32)
+        mine += jnp.where(core == 0, near[chip, which].astype(jnp.float32), 0.0)
+        for x in range(1, chips):
+            mine += jnp.where(x > chip, far[x, which].astype(jnp.float32), 0.0)
+        out[...] = mine.astype(out.dtype)
+
+    p_first.wait_send()
+    for x in range(chips):
+        @pl.when(x < chip)
+        def _():
+            to_near(x).wait_send()
+            to_far(x).wait_send()
+
+        @pl.when(x != chip)
+        def _():
+            p_to_far(x).wait_send()
+
+    @pl.when(core == 1)
+    def _():
+        to_near(chip).wait_send()
+    p_mine.wait_send()
+    p_theirs.wait_recv()
+
+
+def reduce(gkv, gp):
+    n = gkv.shape[0]
+    chips = n // 2
+    vmem = pl.BlockSpec(memory_space=pltpu.VMEM)
+    piece = gkv.shape[1:]
+    dma = pltpu.SemaphoreType.DMA
+    return pl.pallas_call(
+        functools.partial(reduce_kernel, n),
+        in_specs=[vmem] * 2,
+        out_specs=[vmem] * 3,
+        out_shape=[
+            jax.ShapeDtypeStruct(piece[1:], gkv.dtype),
+            jax.ShapeDtypeStruct(piece[1:], gkv.dtype),
+            jax.ShapeDtypeStruct(gp.shape, gp.dtype),
+        ],
+        scratch_shapes=[
+            pltpu.VMEM((chips,) + piece, gkv.dtype),
+            pltpu.VMEM((chips,) + piece, gkv.dtype),
+            pltpu.VMEM((chips,) + piece, gkv.dtype),
+            pltpu.VMEM(gp.shape[1:], gp.dtype),
+            pltpu.VMEM(gp.shape[1:], gp.dtype),
+            pltpu.VMEM((chips,) + gp.shape[1:], gp.dtype),
+            dma((chips,)), dma((chips,)), dma((chips,)), dma((chips,)),
+            dma((2,)), dma((2,)), dma((chips,)), dma((chips,)),
+        ],
+        compiler_params=pltpu.CompilerParams(
+            collective_id=1, has_side_effects=True, vmem_limit_bytes=32 * 2**20
+        ),
+    )(gkv, gp)
+
+
 def on_device(
     queries, seq_keys, seq_values, out_grad, prefix_keys, prefix_values,
     global_ids, rand_owner, rand_offset, doc_length,
@@ -152,17 +358,16 @@
     tokens, groups, width = seq_keys.shape
     shape = (tokens, groups, queries.shape[1] // groups, width)
     own = jnp.stack([seq_keys, seq_values]).transpose(0, 2, 1, 3)
-    kv = lax.all_gather(own, "seq", axis=0)
+    kv = gather(own, lax.axis_size("seq"))
     o, dq, gkv, gp = attend(
         queries.reshape(shape), out_grad.reshape(shape), kv,
         prefix_keys.transpose(1, 0, 2), prefix_values.transpose(1, 0, 2),
         global_ids, rand_owner, rand_offset, doc_length,
     )
-    mine = lax.psum_scatter(gkv, "seq", scatter_dimension=0)
-    gp = lax.psum(gp, "seq")
-    mine = mine.astype(jnp.bfloat16).transpose(0, 2, 1, 3)
+    gk, gv, gp = reduce(gkv, gp)
+    gk, gv = gk.transpose(1, 0, 2), gv.transpose(1, 0, 2)
     gp = gp.transpose(0, 2, 1, 3)
-    return (o.reshape(queries.shape), dq.reshape(queries.shape), mine[0], mine[1], gp[0], gp[1])
+    return (o.reshape(queries.shape), dq.reshape(queries.shape), gk, gv, gp[0], gp[1])
 
 
 def solution(mesh):

time: 122 us -> 52.6 us (0.43)
  waiting for transfers between devices: 76.6 us -> 0 us
  Pallas kernels: 21.6 us -> 45.1 us
  between operations: 14.4 us -> 1.43 us
  local copies, waits for them, and re-layouts: 7.86 us -> 5.77 us
    psum x1 -> x0, waiting for transfers between devices: 30.8 us -> none  [on_device(): gp = lax.psum(gp, 'seq')]
    reduce_scatter x1 -> x0, waiting for transfers between devices: 25.4 us -> none  [on_device(): mine = lax.psum_scatter(gkv, 'seq', scatter_dimension=0)]
    pallas_call x0 -> x2, Pallas kernels: none -> 23.9 us  [the longest x1 14.6 us: reduce(): pl.pallas_call(functools.partial(reduce_kernel, n), in_specs=[vmem] * 2,...]
    all_gather x1 -> x0, waiting for transfers between devices: 19.8 us -> none  [on_device(): kv = lax.all_gather(own, 'seq', axis=0)]
  transfers between devices with their start and end apart: 3 -> 0, of which waited for: 3 -> 0; matrix products, arithmetic and copies ran while one was open for 2% -> 0% of each run, Pallas kernels for 0% -> 0%
where the time goes in v2:
time: 52.6 us; the launch traced here: 52.3 us
  Pallas kernels  45.1 us (86%)
  local copies, waits for them, and re-layouts  5.77 us (11%)
  between operations  1.43 us (3%)
    pallas_call x1, Pallas kernels, attend(): pl.pallas_call(functools.partial(attend_kernel, per_dev, devices * per_de...  21.3 us
    pallas_call x1, Pallas kernels, reduce(): pl.pallas_call(functools.partial(reduce_kernel, n), in_specs=[vmem] * 2,...  14.6 us
    pallas_call x1, Pallas kernels, gather(): pl.pallas_call(functools.partial(gather_kernel, n), in_specs=[vmem], out_...  9.21 us
    unnamed x18, local copies, waits for them, and re-layouts  3.94 us

profile of v2, /device:TPU:0, one launch (start us, length us, event | category | flops | bytes accessed | tf_op | source)
XLA Modules:
  0.0 52.3 jit_solution(13498378745667854942)
XLA Ops:
  0.6 0.0 copy-start.6
  1.3 0.8 %copy_bitcast_fusion.2 = (bf16[2,64,128]{2,1,0:T(8,128)(2,1)S(1)}, bf16[2,64,128]{2,1,0:T(8,128)(2,1)S(1)}) fusion(bf16[64,2,128]{2,1,0:T(2,128)(2,1)} %param.15, bf16[64,2,128]{2,1,0:T(2,128)(2,1)} %param.14), kind=kLoop, calls=%fused_computation.5 | loop fusion | bytes 131072 | tf_op jit(solution)/shard_map/transpose | solution.py:364
  2.1 0.0 copy-done.6
  2.1 0.0 copy-start.2
  2.1 1.0 %copy_bitcast_fusion = (bf16[1,256,2,128]{3,1,2,0:T(8,128)(2,1)S(1)}, bf16[1,256,2,128]{3,1,2,0:T(8,128)(2,1)S(1)}) fusion(bf16[256,2,128]{2,1,0:T(2,128)(2,1)S(1)} %copy-done.6, bf16[256,2,128]{2,1,0:T(2,128)(2,1)} %param.11), kind=kLoop, calls=%fused_computation.1 | loop fusion | bytes 524288 | tf_op jit(solution)/shard_map/stack | solution.py:360
  3.2 0.0 copy-start.1
  3.2 0.0 copy-start.3
  3.2 0.0 copy-start.4
  3.2 0.0 copy-start.5
  3.3 9.2 %shard_map.145.kv_ref = bf16[4,2,2,256,128]{4,3,2,1,0:T(8,128)(2,1)S(1)} custom-call(bf16[2,2,256,128]{3,2,1,0:T(8,128)(2,1)S(1)} %maximum_bitcast_fusion.own_ref), custom_call_target="tpu_custom_call" | custom-call | tf_op jit(solution)/shard_map/pallas_call | solution.py:209
  12.5 0.0 copy-start
  12.5 1.0 %copy-done = bf16[4,2,2,256,128]{4,3,2,1,0:T(8,128)(2,1)} copy-done((bf16[4,2,2,256,128]{4,3,2,1,0:T(8,128)(2,1)}, bf16[4,2,2,256,128]{4,3,2,1,0:T(8,128)(2,1)S(1)}, u32[]{:S(2)}) %copy-start) | copy-done | bytes 1048600
  13.4 0.0 copy-done.2
  13.4 0.0 copy-done.1
  13.5 0.0 copy-done.3
  13.5 0.0 copy-done.4
  13.5 0.0 copy-done.5
  13.5 21.3 %shard_map.146 = (bf16[256,2,8,128]{3,2,1,0:T(8,128)(2,1)}, bf16[256,2,8,128]{3,2,1,0:T(8,128)(2,1)}, bf16[4,2,2,256,128]{4,3,2,1,0:T(8,128)(2,1)S(1)}, f32[2,2,64,128]{3,2,1,0:T(8,128)S(1)}) custom-call(s32[2]{0:T(128)S(1)} %copy-done.5, s32[2,2]{1,0:T(2,128)S(1)} %copy-done.3, s32[2,2]{1,0:T(2,128)S(1)} %copy-done.4, s32[1]{0:T(128)S(6)} %copy.28.length, ...), custom_call_target="tpu_custom_call" | custom-call | flops 4362076160 | bytes 4194304 | tf_op jit(solution)/shard_map/pallas_call | solution.py:120
  34.7 14.6 %shard_map.147 = (bf16[2,256,128]{2,1,0:T(8,128)(2,1)S(1)}, bf16[2,256,128]{2,1,0:T(8,128)(2,1)S(1)}, f32[2,2,64,128]{3,2,1,0:T(8,128)S(1)}) custom-call(bf16[4,2,2,256,128]{4,3,2,1,0:T(8,128)(2,1)S(1)} %get-tuple-element.15.g_ref, f32[2,2,64,128]{3,2,1,0:T(8,128)S(1)} %get-tuple-element.16.p_ref), custom_call_target="tpu_custom_call" | custom-call | tf_op jit(solution)/shard_map/pallas_call | solution.py:329
  49.4 0.8 %copy.20 = bf16[256,2,128]{2,1,0:T(2,128)(2,1)} copy(bf16[256,2,128]{2,0,1:T(8,128)(2,1)S(1)} %bitcast.23) | data formatting | bytes 262144
  50.2 0.8 %copy.21 = bf16[256,2,128]{2,1,0:T(2,128)(2,1)} copy(bf16[256,2,128]{2,0,1:T(8,128)(2,1)S(1)} %bitcast.22) | data formatting | bytes 262144
  51.0 0.7 %copy.23 = f32[64,2,128]{2,1,0:T(2,128)} copy(f32[64,2,128]{2,0,1:T(8,128)S(1)} %get-tuple-element.26) | data formatting | bytes 131072
  51.6 0.7 %copy.22 = f32[64,2,128]{2,1,0:T(2,128)} copy(f32[64,2,128]{2,0,1:T(8,128)S(1)} %get-tuple-element.27) | data formatting | bytes 131072
  (2 shorter events, 0.0 us)
Async XLA Ops:
  0.6 1.5 %copy-start.6 = (bf16[256,2,128]{2,1,0:T(2,128)(2,1)S(1)}, bf16[256,2,128]{2,1,0:T(2,128)(2,1)}, u32[]{:S(2)}) copy-start(bf16[256,2,128]{2,1,0:T(2,128)(2,1)} %param.12) | copy-start | bytes 393220
  2.1 11.3 %copy-start.2 = (bf16[256,16,128]{2,1,0:T(8,128)(2,1)S(1)}, bf16[256,16,128]{2,1,0:T(8,128)(2,1)}, u32[]{:S(2)}) copy-start(bf16[256,16,128]{2,1,0:T(8,128)(2,1)} %param.13) | copy-start | bytes 3145732
  3.2 10.3 %copy-start.1 = (bf16[256,16,128]{2,1,0:T(8,128)(2,1)S(1)}, bf16[256,16,128]{2,1,0:T(8,128)(2,1)}, u32[]{:S(2)}) copy-start(bf16[256,16,128]{2,1,0:T(8,128)(2,1)} %param.10) | copy-start | bytes 3145732
  3.2 10.2 %copy-start.3 = (s32[2,2]{1,0:T(2,128)S(1)}, s32[2,2]{1,0:T(2,128)}, u32[]{:S(2)}) copy-start(s32[2,2]{1,0:T(2,128)} %owner.1) | copy-start | bytes 52
  3.2 10.2 %copy-start.4 = (s32[2,2]{1,0:T(2,128)S(1)}, s32[2,2]{1,0:T(2,128)}, u32[]{:S(2)}) copy-start(s32[2,2]{1,0:T(2,128)} %offset.1) | copy-start | bytes 52
  3.2 10.2 %copy-start.5 = (s32[2]{0:T(128)S(1)}, s32[2]{0:T(128)}, u32[]{:S(2)}) copy-start(s32[2]{0:T(128)} %gids.1) | copy-start | bytes 28
  12.5 1.0 %copy-start = (bf16[4,2,2,256,128]{4,3,2,1,0:T(8,128)(2,1)}, bf16[4,2,2,256,128]{4,3,2,1,0:T(8,128)(2,1)S(1)}, u32[]{:S(2)}) copy-start(bf16[4,2,2,256,128]{4,3,2,1,0:T(8,128)(2,1)S(1)} %shard_map.145.kv_ref) | copy-start | bytes 3145732

commit v3 on v2

--- a/solution.py
+++ b/solution.py
@@ -9,7 +9,7 @@
 from jax.sharding import PartitionSpec as P
 
 BLK = 128
-LANES = 256
+LANES = 1024
 MESH = pl.DeviceIdType.MESH
 masked_score = -1e30
 
@@ -32,76 +32,93 @@
     i = lax.axis_index("seq") * per_dev + b
     doc = length[0]
 
-    entries = [i - 1, i]
+    entries = [i, i - 1]
     entries += [gids[j] for j in range(gids.shape[0])]
     entries += [owner[b, j] * per_dev + offset[b, j] for j in range(owner.shape[1])]
-    places, limits = [], []
+    slots = len(entries)
+    places, count = [i] * slots, 0
     for j, e in enumerate(entries):
-        ok = (e >= 0) & (e <= i)
+        ok = (e >= 0) & (e <= i) & (e * BLK < doc)
         for earlier in entries[:j]:
             ok = ok & (e != earlier)
-        places.append(jnp.where(ok, e, i))
-        limits.append(jnp.where(ok, doc - e * BLK, 0))
+        for k in range(j + 1):
+            places[k] = jnp.where(ok & (count == k), e, places[k])
+        count = count + ok.astype(jnp.int32)
 
     @pl.when((b == 0) & (g == 0))
     def _():
         acc[...] = jnp.zeros_like(acc)
         gp_ref[...] = jnp.zeros_like(gp_ref)
 
-    k_s[0:psz, :] = pk_ref[g]
-    v_s[0:psz, :] = pv_ref[g]
-    for j, e in enumerate(places):
-        at = pl.ds(psz + j * BLK, BLK)
-        dev = e // per_dev
-        inner = pl.ds(pl.multiple_of((e - dev * per_dev) * BLK, BLK), BLK)
-        k_s[at, :] = kv_ref[dev, 0, g, inner, :]
-        v_s[at, :] = kv_ref[dev, 1, g, inner, :]
-
-    keys = k_s[...]
-    values = v_s[...]
-    keys_t = keys.T
-    values_t = values.T
-    step = LANES // qheads
-    for c in range(rows // LANES):
-        q = q_ref[c * step : (c + 1) * step, 0].reshape(LANES, width)
-        row_t = i * BLK + c * step + lax.broadcasted_iota(jnp.int32, (LANES, width), 0) // qheads
-        do = do_ref[c * step : (c + 1) * step, 0].reshape(LANES, width)
-        do = jnp.where(row_t < doc, do.astype(jnp.float32), 0.0).astype(jnp.bfloat16)
-        s = dot(keys, q, 1, 1) * (scaling * math.log2(math.e))
-        key_at = lax.broadcasted_iota(jnp.int32, (BLK, LANES), 0)
-        lane_t = c * step + lax.broadcasted_iota(jnp.int32, (BLK, LANES), 1) // qheads
-        parts = [s[0:psz]]
-        for j in range(len(places)):
-            visible = key_at < limits[j]
-            if j == 1:
-                visible = visible & (key_at <= lane_t)
-            parts.append(jnp.where(visible, s[psz + j * BLK : psz + (j + 1) * BLK], masked_score))
-        s = jnp.concatenate(parts, axis=0)
-        w = jnp.exp2(s - jnp.max(s, axis=0, keepdims=True))
-        p = w * (1.0 / jnp.sum(w, axis=0, keepdims=True))
-        p_bf = p.astype(jnp.bfloat16)
-        p_s[:, c * LANES : (c + 1) * LANES] = p_bf
-        dp = dot(values, do, 1, 1)
-        delta = jnp.sum(p * dp, axis=0, keepdims=True)
-        ds = (p * (dp - delta)).astype(jnp.bfloat16)
-        ds_s[:, c * LANES : (c + 1) * LANES] = ds
-        o = dot(values_t, p_bf, 1, 0).T
-        o = jnp.where(row_t < doc, o, 0.0).astype(jnp.bfloat16)
-        o_ref[c * step : (c + 1) * step, 0] = o.reshape(step, qheads, width)
-        dq = (dot(keys_t, ds, 1, 0) * scaling).T.astype(jnp.bfloat16)
-        dq_ref[c * step : (c + 1) * step, 0] = dq.reshape(step, qheads, width)
-
-    all_t = i * BLK + lax.broadcasted_iota(jnp.int32, (rows, width), 0) // qheads
-    do = do_ref[:, 0].reshape(rows, width)
-    do = jnp.where(all_t < doc, do.astype(jnp.float32), 0.0).astype(jnp.bfloat16)
-    gk = dot(ds_s[...], q_ref[:, 0].reshape(rows, width), 1, 0) * scaling
-    gv = dot(p_s[...], do, 1, 0)
-    for which, grad in ((0, gk), (1, gv)):
-        gp_ref[which, g] += grad[0:psz]
-        for j, e in enumerate(places):
+    def work(width_slots):
+        total = psz + width_slots * BLK
+        k_s[0:psz, :] = pk_ref[g]
+        v_s[0:psz, :] = pv_ref[g]
+        for j, e in enumerate(places[:width_slots]):
+            at = pl.ds(psz + j * BLK, BLK)
             dev = e // per_dev
             inner = pl.ds(pl.multiple_of((e - dev * per_dev) * BLK, BLK), BLK)
-            acc[dev, which, g, inner, :] += grad[psz + j * BLK : psz + (j + 1) * BLK]
+            k_s[at, :] = kv_ref[dev, 0, g, inner, :]
+            v_s[at, :] = kv_ref[dev, 1, g, inner, :]
+
+        keys = k_s[0:total, :]
+        values = v_s[0:total, :]
+        keys_t = keys.T
+        values_t = values.T
+        step = LANES // qheads
+        for c in range(rows // LANES):
+            q = q_ref[c * step : (c + 1) * step, 0].reshape(LANES, width)
+            row_t = i * BLK + c * step + lax.broadcasted_iota(jnp.int32, (LANES, width), 0) // qheads
+            do = do_ref[c * step : (c + 1) * step, 0].reshape(LANES, width)
+            do = jnp.where(row_t < doc, do.astype(jnp.float32), 0.0).astype(jnp.bfloat16)
+            s = dot(keys, q, 1, 1) * (scaling * math.log2(math.e))
+            key_at = lax.broadcasted_iota(jnp.int32, (BLK, LANES), 0)
+            lane_t = c * step + lax.broadcasted_iota(jnp.int32, (BLK, LANES), 1) // qheads
+            parts = [s[0:psz]]
+            for j in range(width_slots):
+                visible = key_at < jnp.where(j < count, doc - places[j] * BLK, 0)
+                if j == 0:
+                    visible = visible & (key_at <= lane_t)
+                parts.append(jnp.where(visible, s[psz + j * BLK : psz + (j + 1) * BLK], masked_score))
+            s = jnp.concatenate(parts, axis=0)
+            w = jnp.exp2(s - jnp.max(s, axis=0, keepdims=True))
+            p = w * (1.0 / jnp.sum(w, axis=0, keepdims=True))
+            p_bf = p.astype(jnp.bfloat16)
+            p_s[0:total, c * LANES : (c + 1) * LANES] = p_bf
+            dp = dot(values, do, 1, 1)
+            delta = jnp.sum(p * dp, axis=0, keepdims=True)
+            ds = (p * (dp - delta)).astype(jnp.bfloat16)
+            ds_s[0:total, c * LANES : (c + 1) * LANES] = ds
+            o = dot(values_t, p_bf, 1, 0).T
+            o = jnp.where(row_t < doc, o, 0.0).astype(jnp.bfloat16)
+            o_ref[c * step : (c + 1) * step, 0] = o.reshape(step, qheads, width)
+            dq = (dot(keys_t, ds, 1, 0) * scaling).T.astype(jnp.bfloat16)
+            dq_ref[c * step : (c + 1) * step, 0] = dq.reshape(step, qheads, width)
+
+        all_t = i * BLK + lax.broadcasted_iota(jnp.int32, (rows, width), 0) // qheads
+        do = do_ref[:, 0].reshape(rows, width)
+        do = jnp.where(all_t < doc, do.astype(jnp.float32), 0.0).astype(jnp.bfloat16)
+        gk = dot(ds_s[0:total, :], q_ref[:, 0].reshape(rows, width), 1, 0) * scaling
+        gv = dot(p_s[0:total, :], do, 1, 0)
+        for which, grad in ((0, gk), (1, gv)):
+            gp_ref[which, g] += grad[0:psz]
+            for j, e in enumerate(places[:width_slots]):
+                dev = e // per_dev
+                inner = pl.ds(pl.multiple_of((e - dev * per_dev) * BLK, BLK), BLK)
+                acc[dev, which, g, inner, :] += grad[psz + j * BLK : psz + (j + 1) * BLK]
+
+    fewest = 2
+    for m in range(fewest, slots + 1):
+        fits = (count == m) if m > fewest else (count <= m)
+
+        @pl.when((i * BLK < doc) & fits)
+        def _():
+            work(m)
+
+    @pl.when(i * BLK >= doc)
+    def _():
+        o_ref[...] = jnp.zeros_like(o_ref)
+        dq_ref[...] = jnp.zeros_like(dq_ref)
 
     @pl.when(last)
     def _():

time: 52.6 us -> 44.7 us (0.85)
  the two profiles are of different devices: /device:TPU:0 before, /device:TPU:13 now
where the time goes in v3:
time: 44.7 us; the launch traced here: 44.6 us
  Pallas kernels  37.4 us (84%)
  local copies, waits for them, and re-layouts  5.77 us (13%)
  between operations  1.43 us (3%)
    pallas_call x1, Pallas kernels, reduce(): pl.pallas_call(functools.partial(reduce_kernel, n), in_specs=[vmem] * 2,...  17.2 us
    pallas_call x1, Pallas kernels, attend(): pl.pallas_call(functools.partial(attend_kernel, per_dev, devices * per_de...  12.6 us
    pallas_call x1, Pallas kernels, gather(): pl.pallas_call(functools.partial(gather_kernel, n), in_specs=[vmem], out_...  7.57 us
    unnamed x18, local copies, waits for them, and re-layouts  3.94 us
    another operation x1, local copies, waits for them, and re-layouts, on_device(): own = jnp.stack([seq_keys, seq_values]).transpose(0, 2, 1, 3)  1.03 us

profile of v3, /device:TPU:13, one launch (start us, length us, event | category | flops | bytes accessed | tf_op | source)
XLA Modules:
  0.0 44.6 jit_solution(12214913573965693545)
XLA Ops:
  0.6 0.0 copy-start.6
  1.3 0.8 %copy_bitcast_fusion.2 = (bf16[2,64,128]{2,1,0:T(8,128)(2,1)S(1)}, bf16[2,64,128]{2,1,0:T(8,128)(2,1)S(1)}) fusion(bf16[64,2,128]{2,1,0:T(2,128)(2,1)} %param.15, bf16[64,2,128]{2,1,0:T(2,128)(2,1)} %param.14), kind=kLoop, calls=%fused_computation.5 | loop fusion | bytes 131072 | tf_op jit(solution)/shard_map/transpose | solution.py:381
  2.1 0.0 copy-done.6
  2.1 0.0 copy-start.2
  2.1 1.0 %copy_bitcast_fusion = (bf16[1,256,2,128]{3,1,2,0:T(8,128)(2,1)S(1)}, bf16[1,256,2,128]{3,1,2,0:T(8,128)(2,1)S(1)}) fusion(bf16[256,2,128]{2,1,0:T(2,128)(2,1)S(1)} %copy-done.6, bf16[256,2,128]{2,1,0:T(2,128)(2,1)} %param.11), kind=kLoop, calls=%fused_computation.1 | loop fusion | bytes 524288 | tf_op jit(solution)/shard_map/stack | solution.py:377
  3.2 0.0 copy-start.1
  3.2 0.0 copy-start.3
  3.2 0.0 copy-start.4
  3.2 0.0 copy-start.5
  3.3 7.6 %shard_map.145.kv_ref = bf16[4,2,2,256,128]{4,3,2,1,0:T(8,128)(2,1)S(1)} custom-call(bf16[2,2,256,128]{3,2,1,0:T(8,128)(2,1)S(1)} %maximum_bitcast_fusion.own_ref), custom_call_target="tpu_custom_call" | custom-call | tf_op jit(solution)/shard_map/pallas_call | solution.py:226
  10.8 0.0 copy-start
  10.8 1.0 %copy-done = bf16[4,2,2,256,128]{4,3,2,1,0:T(8,128)(2,1)} copy-done((bf16[4,2,2,256,128]{4,3,2,1,0:T(8,128)(2,1)}, bf16[4,2,2,256,128]{4,3,2,1,0:T(8,128)(2,1)S(1)}, u32[]{:S(2)}) %copy-start) | copy-done | bytes 1048600
  11.8 0.0 copy-done.2
  11.8 0.0 copy-done.1
  11.8 0.0 copy-done.3
  11.8 0.0 copy-done.4
  11.8 0.0 copy-done.5
  11.8 12.6 %shard_map.146 = (bf16[256,2,8,128]{3,2,1,0:T(8,128)(2,1)}, bf16[256,2,8,128]{3,2,1,0:T(8,128)(2,1)}, bf16[4,2,2,256,128]{4,3,2,1,0:T(8,128)(2,1)S(1)}, f32[2,2,64,128]{3,2,1,0:T(8,128)S(1)}) custom-call(s32[2]{0:T(128)S(1)} %copy-done.5, s32[2,2]{1,0:T(2,128)S(1)} %copy-done.3, s32[2,2]{1,0:T(2,128)S(1)} %copy-done.4, s32[1]{0:T(128)S(6)} %copy.28.length, ...), custom_call_target="tpu_custom_call" | custom-call | flops 4362076160 | bytes 4194304 | tf_op jit(solution)/shard_map/pallas_call | solution.py:137
  24.4 17.2 %shard_map.147 = (bf16[2,256,128]{2,1,0:T(8,128)(2,1)S(1)}, bf16[2,256,128]{2,1,0:T(8,128)(2,1)S(1)}, f32[2,2,64,128]{3,2,1,0:T(8,128)S(1)}) custom-call(bf16[4,2,2,256,128]{4,3,2,1,0:T(8,128)(2,1)S(1)} %get-tuple-element.15.g_ref, f32[2,2,64,128]{3,2,1,0:T(8,128)S(1)} %get-tuple-element.16.p_ref), custom_call_target="tpu_custom_call" | custom-call | tf_op jit(solution)/shard_map/pallas_call | solution.py:346
  41.7 0.8 %copy.20 = bf16[256,2,128]{2,1,0:T(2,128)(2,1)} copy(bf16[256,2,128]{2,0,1:T(8,128)(2,1)S(1)} %bitcast.23) | data formatting | bytes 262144
  42.4 0.8 %copy.21 = bf16[256,2,128]{2,1,0:T(2,128)(2,1)} copy(bf16[256,2,128]{2,0,1:T(8,128)(2,1)S(1)} %bitcast.22) | data formatting | bytes 262144
  43.2 0.7 %copy.23 = f32[64,2,128]{2,1,0:T(2,128)} copy(f32[64,2,128]{2,0,1:T(8,128)S(1)} %get-tuple-element.26) | data formatting | bytes 131072
  43.9 0.7 %copy.22 = f32[64,2,128]{2,1,0:T(2,128)} copy(f32[64,2,128]{2,0,1:T(8,128)S(1)} %get-tuple-element.27) | data formatting | bytes 131072
  (2 shorter events, 0.0 us)
Async XLA Ops:
  0.6 1.5 %copy-start.6 = (bf16[256,2,128]{2,1,0:T(2,128)(2,1)S(1)}, bf16[256,2,128]{2,1,0:T(2,128)(2,1)}, u32[]{:S(2)}) copy-start(bf16[256,2,128]{2,1,0:T(2,128)(2,1)} %param.12) | copy-start | bytes 393220
  2.1 9.7 %copy-start.2 = (bf16[256,16,128]{2,1,0:T(8,128)(2,1)S(1)}, bf16[256,16,128]{2,1,0:T(8,128)(2,1)}, u32[]{:S(2)}) copy-start(bf16[256,16,128]{2,1,0:T(8,128)(2,1)} %param.13) | copy-start | bytes 3145732
  3.2 8.6 %copy-start.1 = (bf16[256,16,128]{2,1,0:T(8,128)(2,1)S(1)}, bf16[256,16,128]{2,1,0:T(8,128)(2,1)}, u32[]{:S(2)}) copy-start(bf16[256,16,128]{2,1,0:T(8,128)(2,1)} %param.10) | copy-start | bytes 3145732
  3.2 8.6 %copy-start.3 = (s32[2,2]{1,0:T(2,128)S(1)}, s32[2,2]{1,0:T(2,128)}, u32[]{:S(2)}) copy-start(s32[2,2]{1,0:T(2,128)} %owner.1) | copy-start | bytes 52
  3.2 8.6 %copy-start.4 = (s32[2,2]{1,0:T(2,128)S(1)}, s32[2,2]{1,0:T(2,128)}, u32[]{:S(2)}) copy-start(s32[2,2]{1,0:T(2,128)} %offset.1) | copy-start | bytes 52
  3.2 8.6 %copy-start.5 = (s32[2]{0:T(128)S(1)}, s32[2]{0:T(128)}, u32[]{:S(2)}) copy-start(s32[2]{0:T(128)} %gids.1) | copy-start | bytes 28
  10.8 1.0 %copy-start = (bf16[4,2,2,256,128]{4,3,2,1,0:T(8,128)(2,1)}, bf16[4,2,2,256,128]{4,3,2,1,0:T(8,128)(2,1)S(1)}, u32[]{:S(2)}) copy-start(bf16[4,2,2,256,128]{4,3,2,1,0:T(8,128)(2,1)S(1)} %shard_map.145.kv_ref) | copy-start | bytes 3145732
